TPU v7x, 256 devices: a whole 4x4x8 slice. The times are simulated.
256 devices in a mesh: dp: 32 (over z, y), freq: 8 (over x, core).
Axes of the slice: x: 4, y: 4, z: 8, core: 2. Of those that a mesh axis runs over, the one named last changes fastest.
Arguments:
- inputs: bfloat16 [32768, 128], P('dp'), may hold values from -6 to 6
- freqs: bfloat16 [128, 32768], P(None, 'freq'), may hold values from -1.5 to 1.5
- targets: bfloat16 [32768, 64], P('dp'), may hold values from -6 to 6
- counts: int32 [32], P('dp'), may hold values from 256 to 1024, as said below
Outputs:
- weights: float32 [2, 32768, 64], P(None, 'freq')
Inputs may be any that keep to these rules, and one draw needn't show every extreme that they name: `counts`: some index of dp has all 1024 slots valid and some has a quarter of them.
All inputs are finite; a program needn't handle non-finite values.
Results may differ from a plain program's by a relative error of at most 0.0031.
Values may be sent and summed in bfloat16 or wider, within the bound.
A program may use at most 64 MiB of HBM per device.

v0:
```python
import jax
import jax.numpy as jnp
from jax import lax
from jax.sharding import PartitionSpec as P

PAIRS = 32768
ITERS = 2


RIDGE = 0.5


def per_device(inputs, freqs, targets, counts):
    rows = inputs.shape[0]
    scale = PAIRS ** (-0.5)
    slots = lax.iota(jnp.int32, rows)
    live = (slots < counts[0]).astype(jnp.float32)[:, None] * scale

    def make_tile():
        phase = jnp.dot(inputs, freqs, preferred_element_type=jnp.float32)
        return jnp.stack([jnp.cos(phase) * live, jnp.sin(phase) * live]).astype(jnp.bfloat16)

    def current_tile():
        return make_tile()

    def back_project(tile, values):
        terms = jnp.einsum("crp,rk->cpk", tile, values, preferred_element_type=jnp.float32)
        return lax.psum_scatter(terms, "dp", scatter_dimension=1, tiled=True)

    def reduce_dots(values):
        return lax.psum(values, ("dp", "freq"))

    def squares(values):
        return jnp.sum(values * values, axis=(0, 1))

    right = back_project(current_tile(), targets)
    weights = jnp.zeros_like(right)
    residual = right
    direction = right
    norm_now = reduce_dots(squares(residual))
    for step in range(ITERS):
        apply_tile = current_tile()
        lowered = direction.astype(jnp.bfloat16)
        whole = lax.all_gather(lowered, "dp", axis=1, tiled=True)
        partial_value = jnp.einsum(
            "crp,cpk->rk", apply_tile, whole, preferred_element_type=jnp.float32
        )
        images = lax.psum(partial_value.astype(jnp.bfloat16), "freq")
        image = back_project(apply_tile, images) + RIDGE * direction
        alpha = norm_now / reduce_dots(jnp.sum(direction * image, axis=(0, 1)))
        weights = weights + alpha * direction
        residual = residual - alpha * image
        fresh = reduce_dots(squares(residual))
        direction = residual + fresh / norm_now * direction
        norm_now = fresh
    return lax.all_gather(weights, "dp", axis=1, tiled=True)


def solution(mesh):
    return jax.shard_map(
        per_device,
        mesh=mesh,
        in_specs=(P("dp", None), P(None, "freq"), P("dp", None), P("dp")),
        out_specs=P(None, "freq", None),
        check_vma=False,
    )
```

profile of v0, /device:TPU:1, one launch (start us, length us, event | category | flops | bytes accessed | tf_op | source)
XLA Modules:
  0.0 1341.1 jit_solution(10127060768445949424)
XLA Ops:
  7.8 63.1 %fusion = (bf16[1,1024,4096]{2,1,0:T(8,128)(2,1)S(1)}, bf16[1,1024,4096]{2,1,0:T(8,128)(2,1)S(1)}) fusion(f32[1024]{0:T(1024)S(1)} %fusion.10, bf16[1024,128]{1,0:T(8,128)(2,1)} %param.4, bf16[128,4096]{1,0:T(8,128)(2,1)S(1)} %copy-done), kind=kOutput, calls=%fused_computation.3 | convolution fusion | flops 1090519040 | bytes 18092032 | tf_op jit(solution)/shard_map/dot_general | solution.py:20
  70.9 3.2 copy-done.1
  74.1 2.5 copy-done.2
  76.6 4.2 fusion.8
  80.9 215.1 %reduce-scatter.4.cloned.1.call-done = f32[2,128,64]{1,2,0:T(8,128)} async-done(((f32[2,4096,64]{1,2,0:T(8,128)}), f32[2,128,64]{1,2,0:T(8,128)}) %reduce-scatter.4.cloned.1.call-update) | async-done | bytes 65552 | tf_op jit(solution)/shard_map/reduce_scatter | solution.py:28
  296.0 1.5 convert_element_type.17
  297.5 71.7 %all-gather.4.cloned.1.call-done = bf16[2,4096,64]{1,2,0:T(8,128)(2,1)} async-done(((bf16[2,128,64]{1,2,0:T(8,128)(2,1)}), bf16[2,4096,64]{1,2,0:T(8,128)(2,1)}) %all-gather.4.cloned.1.call-update) | async-done | bytes 1048592 | tf_op jit(solution)/shard_map/all_gather | solution.py:44
  369.3 9.6 fusion.2
  379.0 65.2 %all-reduce.4.cloned.1.call-done = bf16[1024,64]{0,1:T(8,128)(2,1)} async-done(((bf16[1024,64]{0,1:T(8,128)(2,1)}), bf16[1024,64]{0,1:T(8,128)(2,1)}) %all-reduce.4.cloned.1.call-update) | async-done | bytes 131088 | tf_op jit(solution)/shard_map/psum | solution.py:48
  444.3 8.4 fusion.6
  452.8 212.6 %reduce-scatter.6.cloned.1.call-done = f32[2,128,64]{1,2,0:T(8,128)} async-done(((f32[2,4096,64]{1,2,0:T(8,128)}), f32[2,128,64]{1,2,0:T(8,128)}) %reduce-scatter.6.cloned.1.call-update) | async-done | bytes 65552 | tf_op jit(solution)/shard_map/reduce_scatter | solution.py:28
  666.3 79.4 %all-reduce = (f32[64]{0:T(128)S(1)}, f32[64]{0:T(128)S(1)}) all-reduce(f32[64]{0:T(128)S(1)} %get-tuple-element.6, f32[64]{0:T(128)S(1)} %get-tuple-element.5), channel_id=1, replica_groups=mesh['dp'=32,'freq'=8] {'dp','freq'}, use_global_device_ids=true, to_apply=%region_2.0 | all-reduce | flops 128 | bytes 1024 | tf_op jit(solution)/shard_map/psum | solution.py:31
  745.8 1.0 multiply_reduce_fusion.1
  746.8 73.3 %psum.45 = f32[64]{0:T(128)S(1)} all-reduce(f32[64]{0:T(128)S(1)} %multiply_reduce_fusion.1), channel_id=1, replica_groups=mesh['dp'=32,'freq'=8] {'dp','freq'}, use_global_device_ids=true, to_apply=%region_8.0 | all-reduce | flops 64 | bytes 512 | tf_op jit(solution)/shard_map/psum | solution.py:31
  820.1 1.5 fusion.11
  821.9 63.4 %all-gather.6.cloned.1.call-done = bf16[2,4096,64]{1,2,0:T(8,128)(2,1)} async-done(((bf16[2,128,64]{1,2,0:T(8,128)(2,1)}), bf16[2,4096,64]{1,2,0:T(8,128)(2,1)}) %all-gather.6.cloned.1.call-update) | async-done | bytes 1048592 | tf_op jit(solution)/shard_map/all_gather | solution.py:44
  885.3 9.6 fusion.3
  895.0 65.3 %all-reduce.6.cloned.1.call-done = bf16[1024,64]{0,1:T(8,128)(2,1)} async-done(((bf16[1024,64]{0,1:T(8,128)(2,1)}), bf16[1024,64]{0,1:T(8,128)(2,1)}) %all-reduce.6.cloned.1.call-update) | async-done | bytes 131088 | tf_op jit(solution)/shard_map/psum | solution.py:48
  960.3 8.4 fusion.4
  968.8 212.6 %reduce-scatter.8.cloned.1.call-done = f32[2,128,64]{1,2,0:T(8,128)} async-done(((f32[2,4096,64]{1,2,0:T(8,128)}), f32[2,128,64]{1,2,0:T(8,128)}) %reduce-scatter.8.cloned.1.call-update) | async-done | bytes 65552 | tf_op jit(solution)/shard_map/reduce_scatter | solution.py:28
  1181.5 1.0 multiply_reduce_fusion
  1182.5 79.4 %psum.47 = f32[64]{0:T(128)S(1)} all-reduce(f32[64]{0:T(128)S(1)} %multiply_reduce_fusion), channel_id=1, replica_groups=mesh['dp'=32,'freq'=8] {'dp','freq'}, use_global_device_ids=true, to_apply=%region_12.0 | all-reduce | flops 64 | bytes 512 | tf_op jit(solution)/shard_map/psum | solution.py:31
  1262.6 68.5 %all-gather.8.cloned.1.call-done = f32[2,4096,64]{1,2,0:T(8,128)} async-done(((f32[2,128,64]{1,2,0:T(8,128)}), f32[2,4096,64]{1,2,0:T(8,128)}) %all-gather.8.cloned.1.call-update) | async-done | bytes 2097168 | tf_op jit(solution)/shard_map/all_gather | solution.py:56
  1331.1 3.1 copy.9
  (32 shorter events, 2.8 us)
Async XLA Ops:
  6.5 1.2 copy-start
  6.5 289.5 %reduce-scatter.4.cloned.1.call-start = ((), (), s32[]{:S(2)}) async-start(), calls=%async_computation.3 | async-start | bytes 2162688 | tf_op jit(solution)/shard_map/reduce_scatter | solution.py:28
  7.8 68.9 %copy-start.5 = (bf16[1024,64]{0,1:T(8,128)(2,1)S(1)}, bf16[1024,64]{0,1:T(8,128)(2,1)}, u32[]{:S(2)}) copy-start(bf16[1024,64]{0,1:T(8,128)(2,1)} %param.6) | copy-start | bytes 393220
  70.9 3.2 copy-start.1
  70.9 5.7 copy-start.2
  80.9 288.4 %all-gather.4.cloned.1.call-start = ((), (), s32[]{:S(2)}) async-start(), calls=%async_computation.4 | async-start | bytes 1081344 | tf_op jit(solution)/shard_map/all_gather | solution.py:44
  297.5 146.8 %all-reduce.4.cloned.1.call-start = ((), (), s32[]{:S(2)}) async-start(), calls=%async_computation.5 | async-start | bytes 262144 | tf_op jit(solution)/shard_map/psum | solution.py:48
  378.9 286.4 %copy-start.3 = (f32[2,128,64]{1,2,0:T(8,128)S(1)}, f32[2,128,64]{1,2,0:T(8,128)}, u32[]{:S(2)}) copy-start(f32[2,128,64]{1,2,0:T(8,128)} %reduce-scatter.4.cloned.1.call-done) | copy-start | bytes 196612
  379.0 286.4 %reduce-scatter.6.cloned.1.call-start = ((), (), s32[]{:S(2)}) async-start(), calls=%async_computation.6 | async-start | bytes 2162688 | tf_op jit(solution)/shard_map/reduce_scatter | solution.py:28
  452.7 432.6 %all-gather.6.cloned.1.call-start = ((), (), s32[]{:S(2)}) async-start(), calls=%async_computation.7 | async-start | bytes 1081344 | tf_op jit(solution)/shard_map/all_gather | solution.py:44
  821.7 138.7 %all-reduce.6.cloned.1.call-start = ((), (), s32[]{:S(2)}) async-start(), calls=%async_computation.8 | async-start | bytes 262144 | tf_op jit(solution)/shard_map/psum | solution.py:48
  895.0 286.5 %copy-start.4 = (f32[2,128,64]{1,2,0:T(8,128)S(1)}, f32[2,128,64]{1,2,0:T(8,128)}, u32[]{:S(2)}) copy-start(f32[2,128,64]{1,2,0:T(8,128)} %reduce-scatter.6.cloned.1.call-done) | copy-start | bytes 196612
  895.0 286.5 %reduce-scatter.8.cloned.1.call-start = ((), (), s32[]{:S(2)}) async-start(), calls=%async_computation.9 | async-start | bytes 2162688 | tf_op jit(solution)/shard_map/reduce_scatter | solution.py:28
  968.8 362.4 %all-gather.8.cloned.1.call-start = ((), (), s32[]{:S(2)}) async-start(), calls=%async_computation.10 | async-start | bytes 2162688 | tf_op jit(solution)/shard_map/all_gather | solution.py:56
Sparse Core Ops, SparseCore 0:
  81.0 214.9 reduce-scatter.3
  298.8 70.4 all-gather.3
  379.1 65.1 all-reduce.3
  452.8 212.4 reduce-scatter.5
  821.8 63.5 all-gather.5
  895.1 65.1 all-reduce.5
  968.9 212.5 reduce-scatter.7
  1262.8 68.3 all-gather.7
where the time goes:
time: 1340 us
  waiting for transfers between devices  975 us (73%)
  blocking collectives  232 us (17%)
  matrix products  103 us (8%)
  between operations  14.3 us (1%)
    reduce_scatter x3, waiting for transfers between devices, back_project(): return lax.psum_scatter(terms, 'dp', scatter_dimension=1, tiled=True)  640 us
    psum x3, blocking collectives, reduce_dots(): return lax.psum(values, ('dp', 'freq'))  232 us
    all_gather x2, waiting for transfers between devices, per_device(): whole = lax.all_gather(lowered, 'dp', axis=1, tiled=True)  135 us
    psum x2, waiting for transfers between devices, per_device(): images = lax.psum(partial_value.astype(jnp.bfloat16), 'freq')  131 us
    all_gather x1, waiting for transfers between devices, per_device(): return lax.all_gather(weights, 'dp', axis=1, tiled=True)  68.5 us
    dot_general x1, matrix products, make_tile(): phase = jnp.dot(inputs, freqs, preferred_element_type=jnp.float32)  63.1 us
  transfers between devices with their start and end apart: 8, of which 8 were waited for; matrix products, arithmetic and copies ran while one was open for 0% of the time, Pallas kernels for 0%

commit v1 on v0

v1 whole, which is shorter than its diff:
```python
import functools
import math

import jax
import jax.numpy as jnp
from jax import lax
from jax.experimental import pallas as pl
from jax.experimental.pallas import tpu as pltpu
from jax.sharding import PartitionSpec as P

MESH = pl.DeviceIdType.MESH
RIDGE = 0.5
NY = 4
ROWT = 128

SIN_HALF = (3.14159258, -5.16770687, 2.55003119, -0.598044194, 0.0772183862)
COS_HALF = (0.999999953, -4.93479283, 4.05841135, -1.33187657, 0.219689611)
INV_TURN = 0.15915494309189535


def nt_dot(a, b):
    return lax.dot_general(a, b, (((1,), (1,)), ((), ())), preferred_element_type=jnp.float32)


def cos_sin(phase, scale):
    gain = math.sqrt(2.0 * scale)
    turns = phase * INV_TURN
    frac = turns - jnp.round(turns)
    sq = frac * frac
    s = SIN_HALF[4] * gain
    c = COS_HALF[4] * gain
    for i in (3, 2, 1, 0):
        s = s * sq + SIN_HALF[i] * gain
        c = c * sq + COS_HALF[i] * gain
    s = s * frac
    return scale - s * s, s * c


def kernel(nz, nf, scale, count_ref, x_ref, w_ref, y_ref, out_ref, s):
    rows = 128 * nf
    f32, bf16 = jnp.float32, jnp.bfloat16
    dp, me = lax.axis_index("dp"), lax.axis_index("freq")
    z, y = dp // NY, dp % NY
    p1, p2, far = y + 1 - 2 * (y % 2), 3 - y, (y + 2) % NY
    count = count_ref[0]
    T, ph, acc = s["T"], s["ph"], s["acc"]

    def at_y(v):
        return (z * NY + v, me)

    def at_z(v):
        return (v * NY + y, me)

    def at_f(v):
        return (dp, v)

    barrier = pltpu.get_barrier_semaphore()
    peers = [at_y((y + d) % NY) for d in range(1, NY)]
    peers += [at_z((z + d) % nz) for d in range(1, nz)]
    peers += [at_f((me + d) % nf) for d in range(1, nf)]
    for peer in peers:
        pl.semaphore_signal(barrier, inc=1, device_id=peer, device_id_type=MESH)

    started = []
    used = [0]

    def push(src, dst, peer):
        k = used[0]
        used[0] += 1
        copy = pltpu.make_async_remote_copy(
            src_ref=src, dst_ref=dst, send_sem=s["send"].at[k], recv_sem=s["recv"].at[k],
            device_id=peer, device_id_type=MESH)
        copy.start()
        started.append(copy)
        return copy

    lane = lax.broadcasted_iota(jnp.int32, (64, rows), 1)
    s["yb"][...] = jnp.where(lane < count, y_ref[...].astype(f32), 0.0).astype(bf16)

    def features(yd):
        def block(j, _):
            chunk = yd * nz + 2 * j
            off = pl.multiple_of(chunk * 128, 128)
            ph[...] = jnp.dot(x_ref[...], w_ref[:, pl.ds(off, 256)], preferred_element_type=f32)

            def tile(i, _):
                r = pl.ds(pl.multiple_of(i * ROWT, ROWT), ROWT)
                c, v = cos_sin(ph[r, :], scale)
                c, v = c.astype(bf16), v.astype(bf16)
                for h in range(2):
                    T[chunk + h, r, 0:128] = c[:, 128 * h:128 * h + 128]
                    T[chunk + h, r, 128:256] = v[:, 128 * h:128 * h + 128]
                return 0

            lax.fori_loop(0, rows // ROWT, tile, 0)
            return 0

        lax.fori_loop(0, nz // 2, block, 0)

    def back(yd, rhs, own, low):
        step = min(4, nz)

        def block(j, _):
            for h in range(step):
                zd = step * j + h
                v = jnp.dot(rhs[...], T[yd * nz + zd], preferred_element_type=f32)
                for c in range(2):
                    own[c, yd, zd] = v[:, 128 * c:128 * c + 128]
                    if low is not None:
                        low[c, yd, zd] = v[:, 128 * c:128 * c + 128].astype(bf16)
            return 0

        lax.fori_loop(0, nz // step, block, 0)

    def back_reduce(tag, rhs, with_features):
        own, low = s["own"], None
        if tag == "g":
            low = s["low"]
        out = own if low is None else low
        r1, r2, st, tot, zr = (s[k + tag] for k in ("r1", "r2", "st", "tot", "zr"))
        kind = st.dtype

        def group(yd):
            if with_features:
                features(yd)
            back(yd, rhs, own, low)

        def fold(c, yd, got):
            def add(i, _):
                st[c, i] = (own[c, yd, i] + r1[c, 0, i].astype(f32)).astype(kind)
                return 0

            lax.fori_loop(0, nz, add, 0)

        group(far)
        if with_features:
            pl.semaphore_wait(barrier, len(peers))
        a0 = push(out.at[0, far], r1.at[0, 0], at_y(p1))
        b0 = push(out.at[1, far], r1.at[1, 0], at_y(p2))
        group(p1)
        a1 = push(out.at[0, p1], r1.at[0, 1], at_y(p1))
        b0.wait_recv()
        fold(1, p1, b0)
        b2 = push(st.at[1], r2.at[1], at_y(p1))
        group(p2)
        b1 = push(out.at[1, p2], r1.at[1, 1], at_y(p2))
        a0.wait_recv()
        fold(0, p2, a0)
        a2 = push(st.at[0], r2.at[0], at_y(p2))
        group(y)
        for copy in (a1, b2, b1, a2):
            copy.wait_recv()

        def total(zd):
            return [own[c, y, zd] + r1[c, 1, zd].astype(f32) + r2[c, zd].astype(f32) for c in range(2)]

        arriving = []
        for d in range(1, nz):
            zd = (z + d) % nz
            for c, v in enumerate(total(zd)):
                tot[d, c] = v.astype(kind)
            arriving.append(push(tot.at[d], zr.at[d], at_z(zd)))
        value = total(z)
        for d, copy in enumerate(arriving):
            copy.wait_recv()
            value = [value[c] + zr[d + 1, c].astype(f32) for c in range(2)]
        return value

    def forward(yd, G, first):
        def block(q, _):
            r = pl.ds(pl.multiple_of(q * 256, 256), 256)
            v = None
            for zd in range(nz):
                g = jnp.concatenate([G[yd, 0, zd], G[yd, 1, zd]], axis=1)
                t = nt_dot(g, T[yd * nz + zd, r, :])
                v = t if v is None else v + t
            for h in range(2):
                part = v[:, 128 * h:128 * h + 128]
                acc[2 * q + h] = part if first else acc[2 * q + h] + part
            return 0

        lax.fori_loop(0, rows // 256, block, 0)

    def gather_forward(tag, value):
        G = s["G" + tag]
        for c in range(2):
            G[y, c, z] = value[c].astype(bf16)
        arriving = []
        for d in range(1, nz):
            arriving.append(push(G.at[y, :, z], G.at[y, :, z], at_z((z + d) % nz)))
        for copy in arriving:
            copy.wait_recv()
        g1 = push(G.at[y], G.at[y], at_y(p1))
        g2 = push(G.at[y], G.at[y], at_y(p2))
        forward(y, G, True)
        g1.wait_recv()
        g2.wait_recv()
        h1 = push(G.at[p2, 0], G.at[p2, 0], at_y(p1))
        h2 = push(G.at[p1, 1], G.at[p1, 1], at_y(p2))
        forward(p1, G, False)
        forward(p2, G, False)
        h1.wait_recv()
        h2.wait_recv()
        forward(far, G, False)
        up, ur = s["up" + tag], s["ur" + tag]
        arriving = []
        for d in range(1, nf):
            to = (me + d) % nf
            up[d] = acc[to].astype(up.dtype)
            arriving.append(push(up.at[d], ur.at[d], at_f(to)))
        total = acc[me]
        for d, copy in enumerate(arriving):
            copy.wait_recv()
            total = total + ur[d + 1].astype(f32)
        slot = me * 128 + lax.broadcasted_iota(jnp.int32, (64, 128), 1)
        return jnp.where(slot < count, total, 0.0)

    def pack(tag, columns):
        at = lax.broadcasted_iota(jnp.int32, (64, 128), 1)
        tile = jnp.zeros((64, 128), f32)
        for k, v in enumerate(columns):
            tile = jnp.where(at == k, v, tile)
        s["sc" + tag][0, :, 0:64] = tile.T[0:8, :]

    def dots(pairs):
        return sum(jnp.sum(a * b, axis=1, keepdims=True) for a, b in pairs)

    def scalar_stage(tag, stage, targets):
        n = len(targets)
        sc, sr = s["sc" + tag], s["sr%d" % stage + tag]
        copies = [push(sc.at[stage], sr.at[i], peer) for i, peer in enumerate(targets)]

        def finish():
            v = sc[stage]
            for i, copy in enumerate(copies):
                copy.wait_recv()
                v = v + sr[i]
            sc[stage + 1] = v

        return finish

    to_f = [at_f((me + d) % nf) for d in range(1, nf)]
    to_y = [at_y((y + d) % NY) for d in range(1, NY)]
    to_z = [at_z((z + d) % nz) for d in range(1, nz)]

    def unpack(tag, n):
        v = s["sc" + tag][3]
        v = jnp.concatenate([v] * 16, axis=0).T
        return [v[0:64, k:k + 1] for k in range(n)]

    s["sca"][0] = jnp.zeros((8, 128), f32)
    s["scb"][0] = jnp.zeros((8, 128), f32)

    b = back_reduce("b", s["yb"], True)
    for c in range(2):
        s["bf"][c] = b[c]
    u = gather_forward("b", b)
    s["uf"][...] = u
    s["ui"][me] = u.astype(bf16)
    arriving = [push(s["ui"].at[me], s["ui"].at[me], peer) for peer in to_f]
    b = [s["bf"][c] for c in range(2)]
    pack("a", [dots([(b[0], b[0]), (b[1], b[1])]), dots([(u, u)])])
    finish = scalar_stage("a", 0, to_f)
    for copy in arriving:
        copy.wait_recv()
    for k in range(nf):
        s["yb"][:, 128 * k:128 * k + 128] = s["ui"][k]
    finish()
    finish = scalar_stage("a", 1, to_y)
    while started:
        started.pop(0).wait_send()
    g = back_reduce("g", s["yb"], False)
    finish()
    finish = scalar_stage("a", 2, to_z)
    finish()
    rr, uu = unpack("a", 2)
    alpha0 = rr / (uu + RIDGE * rr)
    b = [s["bf"][c] for c in range(2)]
    r = [(1.0 - RIDGE * alpha0) * b[c] - alpha0 * g[c] for c in range(2)]
    for c in range(2):
        s["rf"][c] = r[c]
    v = gather_forward("g", r)
    u = s["uf"][...]
    b = [s["bf"][c] for c in range(2)]
    r = [s["rf"][c] for c in range(2)]
    pack("b", [dots([(r[0], r[0]), (r[1], r[1])]), dots([(r[0], b[0]), (r[1], b[1])]),
               dots([(v, v)]), dots([(v, u)])])
    scalar_stage("b", 0, to_f)()
    scalar_stage("b", 1, to_y)()
    scalar_stage("b", 2, to_z)()
    fresh, rb, vv, vu = unpack("b", 4)
    rr, uu = unpack("a", 2)
    alpha0 = rr / (uu + RIDGE * rr)
    beta = fresh / rr
    image = vv + 2.0 * beta * vu + beta * beta * uu
    length = fresh + 2.0 * beta * rb + beta * beta * rr
    alpha1 = fresh / (image + RIDGE * length)
    on_b = jnp.broadcast_to(alpha0 + alpha1 * beta, (64, 128))
    on_r = jnp.broadcast_to(alpha1, (64, 128))

    def finish_chunk(k, _):
        at = pl.ds(pl.multiple_of(k * 128, 128), 128)
        for c in range(2):
            out_ref[c, :, at] = (on_b * s["Gb"][k // nz, c, k % nz].astype(f32)
                                 + on_r * s["Gg"][k // nz, c, k % nz].astype(f32))
        return 0

    lax.fori_loop(0, NY * nz, finish_chunk, 0)
    for copy in started:
        copy.wait_send()


def per_device(nz, nf, inputs, freqs, targets, counts):
    rows, pairs = inputs.shape[0], freqs.shape[1]
    f32, bf16 = jnp.float32, jnp.bfloat16
    copies = 2 * (6 + 2 * (nz - 1) + 4 + (nf - 1)) + (nf - 1) + 2 * (nf - 1 + NY - 1 + nz - 1)
    vmem = pltpu.VMEM
    scratch = {
        "T": vmem((NY * nz, rows, 256), bf16),
        "ph": vmem((rows, 256), f32),
        "acc": vmem((nf, 64, 128), f32),
        "yb": vmem((64, rows), bf16),
        "own": vmem((2, NY, nz, 64, 128), f32),
        "low": vmem((2, NY, nz, 64, 128), bf16),
        "bf": vmem((2, 64, 128), f32),
        "rf": vmem((2, 64, 128), f32),
        "uf": vmem((64, 128), f32),
        "ui": vmem((nf, 64, 128), bf16),
        "send": pltpu.SemaphoreType.DMA((copies,)),
        "recv": pltpu.SemaphoreType.DMA((copies,)),
    }
    for tag, kind in (("b", f32), ("g", bf16)):
        scratch["r1" + tag] = vmem((2, 2, nz, 64, 128), kind)
        scratch["r2" + tag] = vmem((2, nz, 64, 128), kind)
        scratch["st" + tag] = vmem((2, nz, 64, 128), kind)
        scratch["tot" + tag] = vmem((nz, 2, 64, 128), kind)
        scratch["zr" + tag] = vmem((nz, 2, 64, 128), kind)
        scratch["G" + tag] = vmem((NY, 2, nz, 64, 128), bf16)
        scratch["up" + tag] = vmem((nf, 64, 128), bf16)
        scratch["ur" + tag] = vmem((nf, 64, 128), bf16)
    for tag in ("a", "b"):
        scratch["sc" + tag] = vmem((4, 8, 128), f32)
        for stage, n in enumerate((nf, NY, nz)):
            scratch["sr%d" % stage + tag] = vmem((n, 8, 128), f32)
    whole = pl.BlockSpec(memory_space=pltpu.VMEM)
    out = pl.pallas_call(
        functools.partial(kernel, nz, nf, float(pairs * nf) ** -0.5),
        out_shape=jax.ShapeDtypeStruct((2, 64, pairs), f32),
        in_specs=[pl.BlockSpec(memory_space=pltpu.SMEM), whole, whole, whole],
        out_specs=whole,
        scratch_shapes=[scratch],
        compiler_params=pltpu.CompilerParams(
            collective_id=0, has_side_effects=True, vmem_limit_bytes=56 * 2 ** 20),
        cost_estimate=pl.CostEstimate(
            flops=12 * rows * pairs * 64, bytes_accessed=4 * 2 ** 20, transcendentals=0),
    )(counts, inputs, freqs, targets.T)
    return jnp.swapaxes(out, 1, 2)


def solution(mesh):
    nz, nf = mesh.shape["dp"] // NY, mesh.shape["freq"]
    return jax.shard_map(
        functools.partial(per_device, nz, nf),
        mesh=mesh,
        in_specs=(P("dp", None), P(None, "freq"), P("dp", None), P("dp")),
        out_specs=P(None, "freq", None),
        check_vma=False,
    )
```

time: 1340 us -> 155 us (0.12)
  waiting for transfers between devices: 975 us -> 0 us
  blocking collectives: 232 us -> 0 us
  Pallas kernels: 0 us -> 151 us
  matrix products: 103 us -> 0 us
  between operations: 14.3 us -> 0.66 us
    reduce_scatter x3 -> x0, waiting for transfers between devices: 640 us -> none  [back_project(): return lax.psum_scatter(terms, 'dp', scatter_dimension=1, tiled=True)]
    psum x3 -> x0, blocking collectives: 232 us -> none  [reduce_dots(): return lax.psum(values, ('dp', 'freq'))]
    all_gather x3 -> x0, waiting for transfers between devices: 204 us -> none  [the longest x2 135 us: per_device(): whole = lax.all_gather(lowered, 'dp', axis=1, tiled=True)]
    pallas_call x0 -> x1, Pallas kernels: none -> 151 us  [per_device(): pl.pallas_call(functools.partial(kernel, nz, nf, float(pairs * nf) ** (-0...]
    psum x2 -> x0, waiting for transfers between devices: 131 us -> none  [per_device(): images = lax.psum(partial_value.astype(jnp.bfloat16), 'freq')]
    dot_general x6 -> x0, matrix products: 103 us -> none  [the longest x1 63.1 us: make_tile(): phase = jnp.dot(inputs, freqs, preferred_element_type=jnp.float32)]
  transfers between devices with their start and end apart: 8 -> 0, of which waited for: 8 -> 0; matrix products, arithmetic and copies ran while one was open for 0% -> 0% of each run, Pallas kernels for 0% -> 0%
where the time goes in v1:
time: 155 us
  Pallas kernels  151 us (97%)
  local copies, waits for them, and re-layouts  3.11 us (2%)
    pallas_call x1, Pallas kernels, per_device(): pl.pallas_call(functools.partial(kernel, nz, nf, float(pairs * nf) ** (-0...  151 us
    unnamed x1, local copies, waits for them, and re-layouts  3.11 us

profile of v1, /device:TPU:1, one launch (start us, length us, event | category | flops | bytes accessed | tf_op | source)
XLA Modules:
  0.0 154.5 jit_solution(4942591617604195074)
XLA Ops:
  0.7 150.8 %shard_map.46 = f32[2,64,4096]{2,1,0:T(8,128)} custom-call(s32[1]{0:T(128)S(6)} %copy.6.count_ref, bf16[1024,128]{1,0:T(8,128)(2,1)} %x_ref.1, bf16[128,4096]{1,0:T(8,128)(2,1)} %w_ref.1, bf16[64,1024]{1,0:T(8,128)(2,1)} %bitcast.3), custom_call_target="tpu_custom_call" | custom-call | flops 3221225472 | bytes 4194304 | tf_op jit(solution)/shard_map/pallas_call | solution.py:346
  151.4 3.1 %copy.7 = f32[2,4096,64]{1,2,0:T(8,128)} copy(f32[2,4096,64]{1,2,0:T(8,128)} %bitcast.2) | data formatting | bytes 4194304

commit v2 on v1

v2 whole, which is shorter than its diff:
```python
import functools
import math

import jax
import jax.numpy as jnp
from jax import lax
from jax.experimental import pallas as pl
from jax.experimental.pallas import tpu as pltpu
from jax.sharding import PartitionSpec as P

MESH = pl.DeviceIdType.MESH
RIDGE = 0.5
NY = 4
ROWT = 64

SIN_HALF = (3.14158198, -5.1671413, 2.54188707, -0.554608852)
COS_HALF = (0.999999953, -4.93479283, 4.05841135, -1.33187657, 0.219689611)
INV_TURN = 0.15915494309189535


def nt_dot(a, b):
    return lax.dot_general(a, b, (((1,), (1,)), ((), ())), preferred_element_type=jnp.float32)


def cos_sin(phase, scale):
    gain = math.sqrt(2.0 * scale)
    turns = phase * INV_TURN
    frac = turns - jnp.round(turns)
    sq = frac * frac
    s = SIN_HALF[3] * gain
    for i in (2, 1, 0):
        s = s * sq + SIN_HALF[i] * gain
    c = COS_HALF[4] * gain
    for i in (3, 2, 1, 0):
        c = c * sq + COS_HALF[i] * gain
    s = s * frac
    return scale - s * s, s * c


def kernel(nz, nf, scale, count_ref, x_ref, w_ref, y_ref, out_ref, s):
    rows, half = 128 * nf, nz // 2
    rt, rb = rows // 2, min(256, rows)
    f32, bf16 = jnp.float32, jnp.bfloat16
    dp, me = lax.axis_index("dp"), lax.axis_index("freq")
    z, y = dp // NY, dp % NY
    count = count_ref[0]
    T, acc = s["T"], s["acc"]

    def at_y(v):
        return (z * NY + v, me)

    def at_z(v):
        return (v * NY + y, me)

    def at_f(v):
        return (dp, v)

    to_f = [at_f((me + d) % nf) for d in range(1, nf)]
    to_y = [at_y((y + d) % NY) for d in range(1, NY)]
    to_z = [at_z((z + d) % nz) for d in range(1, nz)]
    far_first = sorted(range(1, nz), key=lambda d: -min(d, nz - d))

    barrier = pltpu.get_barrier_semaphore()
    peers = to_f + to_y + to_z
    for peer in peers:
        pl.semaphore_signal(barrier, inc=1, device_id=peer, device_id_type=MESH)

    pending = []
    used = [0]

    def take(n):
        used[0] += n
        return used[0] - n

    def remote(src, dst, peer, k):
        return pltpu.make_async_remote_copy(
            src_ref=src, dst_ref=dst, send_sem=s["send"].at[k], recv_sem=s["recv"].at[k],
            device_id=peer, device_id_type=MESH)

    def push(src, dst, peer):
        copy = remote(src, dst, peer, take(1))
        copy.start()
        pending.append(copy)
        return copy

    lane = lax.broadcasted_iota(jnp.int32, (64, rows), 1)
    s["yb"][...] = jnp.where(lane < count, y_ref[...].astype(f32), 0.0).astype(bf16)

    def chunks(k, j):
        yd = (y + 1 + j) % NY
        return yd * nz + (z + half + k) % nz, yd * nz + (z + half - 1 - k + nz) % nz

    def back_reducer(tag):
        out, own, r1, tot, zr = (s[k + tag] for k in ("out", "own", "r1", "tot", "zr"))
        base_y, base_z = take(half * (NY - 1)), take(nz)

        def store(k, j, h, v, more):
            for c in range(2):
                part = v[:, 128 * c:128 * c + 128]
                ref = out.at[j, k, h, c] if j < NY - 1 else own.at[k, h, c]
                if more:
                    part = part + ref[...].astype(f32)
                ref[...] = part.astype(ref.dtype)

        def y_copy(k, j):
            return remote(out.at[j, k], r1.at[j, k], to_y[j], base_y + k * (NY - 1) + j)

        def z_copy(d):
            return remote(tot.at[d], zr.at[d], at_z((z + d) % nz), base_z + d)

        def sum_y(k, h):
            v = [own[k, h, c] for c in range(2)]
            for j in range(NY - 1):
                v = [v[c] + r1[j, k, h, c].astype(f32) for c in range(2)]
            return v

        def send_z(k, h, d):
            for c, v in enumerate(sum_y(k, h)):
                tot[d, c] = v.astype(tot.dtype)
            z_copy(d).start()

        def wait_y(k):
            for j in range(NY - 1):
                y_copy(k, j).wait_recv()

        def send_batch(k):
            wait_y(k)
            send_z(k, 0, half + k)
            send_z(k, 1, half - 1 - k)

        def last():
            wait_y(half - 1)
            send_z(half - 1, 0, nz - 1)
            value = sum_y(half - 1, 1)
            for d in range(1, nz):
                z_copy(d).wait_recv()
                value = [value[c] + zr[d, c].astype(f32) for c in range(2)]
            for k in range(half):
                for j in range(NY - 1):
                    pending.append(y_copy(k, j))
            for d in range(1, nz):
                pending.append(z_copy(d))
            return value

        return store, y_copy, send_batch, last

    def features_back(tag):
        store, y_copy, send_batch, last = back_reducer(tag)
        phases = (s["ph0"], s["ph1"])

        def phase(k, j, i):
            w = [w_ref[:, pl.ds(pl.multiple_of(c * 128, 128), 128)] for c in chunks(k, j)]
            return jnp.dot(x_ref[rt * i:rt * i + rt, :], jnp.concatenate(w, axis=1),
                           preferred_element_type=f32)

        def back(k, j, i):
            for h, chunk in enumerate(chunks(k, j)):
                v = jnp.dot(s["yb"][:, rt * i:rt * i + rt], T[chunk, rt * i:rt * i + rt, :],
                            preferred_element_type=f32)
                store(k, j, h, v, i > 0)

        for chunk in chunks(0, NY - 1):
            T[chunk] = jnp.zeros((rows, 256), bf16)
        phases[0][...] = phase(0, 0, 0)

        def batch(k, _):
            for j in range(NY):
                pk, pj = (k, j - 1) if j else (jnp.maximum(k - 1, 0), NY - 1)
                nk, nj = (k, j + 1) if j < NY - 1 else ((k + 1) % half, 0)
                here = chunks(k, j)
                for i in range(2):
                    back(pk, pj, i)
                    phases[1 - i][...] = phase(k, j, 1) if i == 0 else phase(nk, nj, 0)
                    for r in range(0, rt, ROWT):
                        c, v = cos_sin(phases[i][r:r + ROWT, :], scale)
                        c, v = c.astype(bf16), v.astype(bf16)
                        for h in range(2):
                            at = pl.ds(rt * i + r, ROWT)
                            T[here[h], at, 0:128] = c[:, 128 * h:128 * h + 128]
                            T[here[h], at, 128:256] = v[:, 128 * h:128 * h + 128]
                if j == 1:
                    @pl.when(k == 0)
                    def _():
                        pl.semaphore_wait(barrier, len(peers))
                if j:
                    y_copy(k, j - 1).start()
            pl.when(k > 0)(lambda: send_batch(k - 1))
            return 0

        lax.fori_loop(0, half, batch, 0)
        for i in range(2):
            back(half - 1, NY - 1, i)
        return last()

    def only_back(tag, rhs, between):
        store, y_copy, send_batch, last = back_reducer(tag)

        def batch(k, _):
            for j in range(NY):
                for h, chunk in enumerate(chunks(k, j)):
                    store(k, j, h, jnp.dot(rhs[...], T[chunk], preferred_element_type=f32), False)
                if j < NY - 1:
                    y_copy(k, j).start()
            return 0

        lax.fori_loop(0, half, batch, 0)
        between()

        def sums(k, _):
            send_batch(k)
            return 0

        lax.fori_loop(0, half - 1, sums, 0)
        return last()

    def forward(G, which, first=False):
        def block(q, _):
            r = pl.ds(pl.multiple_of(q * rb, rb), rb)
            v = None
            for yd, zd in which:
                g = jnp.concatenate([G[yd, zd, 0], G[yd, zd, 1]], axis=1)
                t = nt_dot(g, T[yd * nz + zd, r, :])
                v = t if v is None else v + t
            for h in range(rb // 128):
                part = v[:, 128 * h:128 * h + 128]
                at = q * (rb // 128) + h
                acc[at] = part if first else acc[at] + part
            return 0

        lax.fori_loop(0, rows // rb, block, 0)

    def gather_forward(tag, value):
        G = s["G" + tag]
        for c in range(2):
            G[y, z, c] = value[c].astype(bf16)
        landing = [push(G.at[y, z], G.at[y, z], to_z[d - 1]) for d in far_first]
        across = [[push(G.at[y, z], G.at[y, z], peer) for peer in to_y]]
        forward(G, [(y, z)], True)
        for copy, d in zip(landing, far_first):
            zd = (z - d + nz) % nz
            copy.wait_recv()
            across.append([push(G.at[y, zd], G.at[y, zd], peer) for peer in to_y])
            forward(G, [(y, zd)])
        for copies, d in zip(across, [0] + far_first):
            for copy in copies:
                copy.wait_recv()
            forward(G, [((y - j + NY) % NY, (z - d + nz) % nz) for j in range(1, NY)])
        up, ur = s["up" + tag], s["ur" + tag]
        arriving = []
        for d in range(1, nf):
            to = (me + d) % nf
            up[d] = acc[to].astype(up.dtype)
            arriving.append(push(up.at[d], ur.at[d], at_f(to)))
        total = acc[me]
        for d, copy in enumerate(arriving):
            copy.wait_recv()
            total = total + ur[d + 1].astype(f32)
        slot = me * 128 + lax.broadcasted_iota(jnp.int32, (64, 128), 1)
        return jnp.where(slot < count, total, 0.0)

    def pack(tag, columns):
        at = lax.broadcasted_iota(jnp.int32, (64, 128), 1)
        tile = jnp.zeros((64, 128), f32)
        for k, v in enumerate(columns):
            tile = jnp.where(at == k, v, tile)
        s["sc" + tag][0, :, 0:64] = tile.T[0:8, :]

    def dots(pairs):
        return sum(jnp.sum(a * b, axis=1, keepdims=True) for a, b in pairs)

    def scalar_stage(tag, stage, targets):
        sc, sr = s["sc" + tag], s["sr%d" % stage + tag]
        copies = [push(sc.at[stage], sr.at[i], peer) for i, peer in enumerate(targets)]

        def finish():
            v = sc[stage]
            for i, copy in enumerate(copies):
                copy.wait_recv()
                v = v + sr[i]
            sc[stage + 1] = v

        return finish

    def unpack(tag, n):
        v = s["sc" + tag][3]
        v = jnp.concatenate([v] * 16, axis=0).T
        return [v[0:64, k:k + 1] for k in range(n)]

    s["sca"][0] = jnp.zeros((8, 128), f32)
    s["scb"][0] = jnp.zeros((8, 128), f32)

    b = features_back("b")
    for c in range(2):
        s["bf"][c] = b[c]
    u = gather_forward("b", b)
    s["uf"][...] = u
    s["ui"][me] = u.astype(bf16)
    arriving = [push(s["ui"].at[me], s["ui"].at[me], peer) for peer in to_f]
    b = [s["bf"][c] for c in range(2)]
    pack("a", [dots([(b[0], b[0]), (b[1], b[1])]), dots([(u, u)])])
    finish = scalar_stage("a", 0, to_f)
    for copy in arriving:
        copy.wait_recv()
    for k in range(nf):
        s["yb"][:, 128 * k:128 * k + 128] = s["ui"][k]
    finish()
    finish = scalar_stage("a", 1, to_y)
    ends = []

    def between():
        finish()
        ends.append(scalar_stage("a", 2, to_z))

    g = only_back("g", s["yb"], between)
    ends[0]()
    rr, uu = unpack("a", 2)
    alpha0 = rr / (uu + RIDGE * rr)
    b = [s["bf"][c] for c in range(2)]
    r = [(1.0 - RIDGE * alpha0) * b[c] - alpha0 * g[c] for c in range(2)]
    for c in range(2):
        s["rf"][c] = r[c]
    v = gather_forward("g", r)
    u = s["uf"][...]
    b = [s["bf"][c] for c in range(2)]
    r = [s["rf"][c] for c in range(2)]
    pack("b", [dots([(r[0], r[0]), (r[1], r[1])]), dots([(r[0], b[0]), (r[1], b[1])]),
               dots([(v, v)]), dots([(v, u)])])
    scalar_stage("b", 0, to_f)()
    scalar_stage("b", 1, to_y)()
    scalar_stage("b", 2, to_z)()
    fresh, rb_, vv, vu = unpack("b", 4)
    rr, uu = unpack("a", 2)
    alpha0 = rr / (uu + RIDGE * rr)
    beta = fresh / rr
    image = vv + 2.0 * beta * vu + beta * beta * uu
    length = fresh + 2.0 * beta * rb_ + beta * beta * rr
    alpha1 = fresh / (image + RIDGE * length)
    on_b = jnp.broadcast_to(alpha0 + alpha1 * beta, (64, 128))
    on_r = jnp.broadcast_to(alpha1, (64, 128))

    def finish_chunk(k, _):
        at = pl.ds(pl.multiple_of(k * 128, 128), 128)
        for c in range(2):
            out_ref[c, :, at] = (on_b * s["Gb"][k // nz, k % nz, c].astype(f32)
                                 + on_r * s["Gg"][k // nz, k % nz, c].astype(f32))
        return 0

    lax.fori_loop(0, NY * nz, finish_chunk, 0)
    for copy in pending:
        copy.wait_send()


def per_device(nz, nf, inputs, freqs, targets, counts):
    rows, pairs = inputs.shape[0], freqs.shape[1]
    f32, bf16 = jnp.float32, jnp.bfloat16
    half = nz // 2
    copies = 2 * (half * (NY - 1) + nz + nz - 1 + nz * (NY - 1) + nf - 1) + nf - 1 + 2 * (nf + NY + nz - 3)
    vmem = pltpu.VMEM
    scratch = {
        "T": vmem((NY * nz, rows, 256), bf16),
        "ph0": vmem((rows // 2, 256), f32),
        "ph1": vmem((rows // 2, 256), f32),
        "acc": vmem((nf, 64, 128), f32),
        "yb": vmem((64, rows), bf16),
        "bf": vmem((2, 64, 128), f32),
        "rf": vmem((2, 64, 128), f32),
        "uf": vmem((64, 128), f32),
        "ui": vmem((nf, 64, 128), bf16),
        "send": pltpu.SemaphoreType.DMA((copies,)),
        "recv": pltpu.SemaphoreType.DMA((copies,)),
    }
    for tag, kind in (("b", f32), ("g", bf16)):
        scratch["out" + tag] = vmem((NY - 1, half, 2, 2, 64, 128), kind)
        scratch["own" + tag] = vmem((half, 2, 2, 64, 128), f32)
        scratch["r1" + tag] = vmem((NY - 1, half, 2, 2, 64, 128), kind)
        scratch["tot" + tag] = vmem((nz, 2, 64, 128), kind)
        scratch["zr" + tag] = vmem((nz, 2, 64, 128), kind)
        scratch["G" + tag] = vmem((NY, nz, 2, 64, 128), bf16)
        scratch["up" + tag] = vmem((nf, 64, 128), bf16)
        scratch["ur" + tag] = vmem((nf, 64, 128), bf16)
    for tag in ("a", "b"):
        scratch["sc" + tag] = vmem((4, 8, 128), f32)
        for stage, n in enumerate((nf, NY, nz)):
            scratch["sr%d" % stage + tag] = vmem((n, 8, 128), f32)
    whole = pl.BlockSpec(memory_space=pltpu.VMEM)
    out = pl.pallas_call(
        functools.partial(kernel, nz, nf, float(pairs * nf) ** -0.5),
        out_shape=jax.ShapeDtypeStruct((2, 64, pairs), f32),
        in_specs=[pl.BlockSpec(memory_space=pltpu.SMEM), whole, whole, whole],
        out_specs=whole,
        scratch_shapes=[scratch],
        compiler_params=pltpu.CompilerParams(
            collective_id=0, has_side_effects=True, vmem_limit_bytes=56 * 2 ** 20),
        cost_estimate=pl.CostEstimate(
            flops=12 * rows * pairs * 64, bytes_accessed=4 * 2 ** 20, transcendentals=0),
    )(counts, inputs, freqs, targets.T)
    return jnp.swapaxes(out, 1, 2)


def solution(mesh):
    nz, nf = mesh.shape["dp"] // NY, mesh.shape["freq"]
    return jax.shard_map(
        functools.partial(per_device, nz, nf),
        mesh=mesh,
        in_specs=(P("dp", None), P(None, "freq"), P("dp", None), P("dp")),
        out_specs=P(None, "freq", None),
        check_vma=False,
    )
```

time: 155 us -> 132 us (0.85)
  Pallas kernels: 151 us -> 128 us
    pallas_call x1, Pallas kernels: 151 us -> 128 us  [per_device(): pl.pallas_call(functools.partial(kernel, nz, nf, float(pairs * nf) ** (-0...]
where the time goes in v2:
time: 132 us
  Pallas kernels  128 us (97%)
  local copies, waits for them, and re-layouts  3.11 us (2%)
    pallas_call x1, Pallas kernels, per_device(): pl.pallas_call(functools.partial(kernel, nz, nf, float(pairs * nf) ** (-0...  128 us
    unnamed x1, local copies, waits for them, and re-layouts  3.11 us

profile of v2, /device:TPU:1, one launch (start us, length us, event | category | flops | bytes accessed | tf_op | source)
XLA Modules:
  0.0 132.2 jit_solution(5648986846507777860)
XLA Ops:
  0.7 128.4 %shard_map.46 = f32[2,64,4096]{2,1,0:T(8,128)} custom-call(s32[1]{0:T(128)S(6)} %copy.6.count_ref, bf16[1024,128]{1,0:T(8,128)(2,1)} %x_ref.1, bf16[128,4096]{1,0:T(8,128)(2,1)} %w_ref.1, bf16[64,1024]{1,0:T(8,128)(2,1)} %bitcast.3), custom_call_target="tpu_custom_call" | custom-call | flops 3221225472 | bytes 4194304 | tf_op jit(solution)/shard_map/pallas_call | solution.py:386
  129.1 3.1 %copy.7 = f32[2,4096,64]{1,2,0:T(8,128)} copy(f32[2,4096,64]{1,2,0:T(8,128)} %bitcast.2) | data formatting | bytes 4194304

commit v3 on v2

--- a/solution.py
+++ b/solution.py
@@ -12,6 +12,7 @@
 RIDGE = 0.5
 NY = 4
 ROWT = 64
+STAGES = {"a": ("f", "y", "z"), "b": ("yf", "z")}
 
 SIN_HALF = (3.14158198, -5.1671413, 2.54188707, -0.554608852)
 COS_HALF = (0.999999953, -4.93479283, 4.05841135, -1.33187657, 0.219689611)
@@ -39,7 +40,7 @@
 
 def kernel(nz, nf, scale, count_ref, x_ref, w_ref, y_ref, out_ref, s):
     rows, half = 128 * nf, nz // 2
-    rt, rb = rows // 2, min(256, rows)
+    rt = rows // 2
     f32, bf16 = jnp.float32, jnp.bfloat16
     dp, me = lax.axis_index("dp"), lax.axis_index("freq")
     z, y = dp // NY, dp % NY
@@ -58,10 +59,11 @@
     to_f = [at_f((me + d) % nf) for d in range(1, nf)]
     to_y = [at_y((y + d) % NY) for d in range(1, NY)]
     to_z = [at_z((z + d) % nz) for d in range(1, nz)]
+    to_yf = [(z * NY + (y + j) % NY, (me + d) % nf) for j in range(NY) for d in range(nf) if j + d]
     far_first = sorted(range(1, nz), key=lambda d: -min(d, nz - d))
 
     barrier = pltpu.get_barrier_semaphore()
-    peers = to_f + to_y + to_z
+    peers = to_yf + to_z
     for peer in peers:
         pl.semaphore_signal(barrier, inc=1, device_id=peer, device_id_type=MESH)
 
@@ -214,20 +216,15 @@
         return last()
 
     def forward(G, which, first=False):
-        def block(q, _):
-            r = pl.ds(pl.multiple_of(q * rb, rb), rb)
-            v = None
-            for yd, zd in which:
-                g = jnp.concatenate([G[yd, zd, 0], G[yd, zd, 1]], axis=1)
-                t = nt_dot(g, T[yd * nz + zd, r, :])
-                v = t if v is None else v + t
-            for h in range(rb // 128):
-                part = v[:, 128 * h:128 * h + 128]
-                at = q * (rb // 128) + h
-                acc[at] = part if first else acc[at] + part
-            return 0
-
-        lax.fori_loop(0, rows // rb, block, 0)
+        v = None
+        for yd, zd in which:
+            g = jnp.concatenate([G[yd, zd, 0], G[yd, zd, 1]], axis=1)
+            t = nt_dot(T[yd * nz + zd], g)
+            v = t if v is None else v + t
+        v = v.T
+        for h in range(nf):
+            part = v[:, 128 * h:128 * h + 128]
+            acc[h] = part if first else acc[h] + part
 
     def gather_forward(tag, value):
         G = s["G" + tag]
@@ -282,7 +279,7 @@
         return finish
 
     def unpack(tag, n):
-        v = s["sc" + tag][3]
+        v = s["sc" + tag][len(STAGES[tag])]
         v = jnp.concatenate([v] * 16, axis=0).T
         return [v[0:64, k:k + 1] for k in range(n)]
 
@@ -325,9 +322,8 @@
     r = [s["rf"][c] for c in range(2)]
     pack("b", [dots([(r[0], r[0]), (r[1], r[1])]), dots([(r[0], b[0]), (r[1], b[1])]),
                dots([(v, v)]), dots([(v, u)])])
-    scalar_stage("b", 0, to_f)()
-    scalar_stage("b", 1, to_y)()
-    scalar_stage("b", 2, to_z)()
+    scalar_stage("b", 0, to_yf)()
+    scalar_stage("b", 1, to_z)()
     fresh, rb_, vv, vu = unpack("b", 4)
     rr, uu = unpack("a", 2)
     alpha0 = rr / (uu + RIDGE * rr)
@@ -354,7 +350,7 @@
     rows, pairs = inputs.shape[0], freqs.shape[1]
     f32, bf16 = jnp.float32, jnp.bfloat16
     half = nz // 2
-    copies = 2 * (half * (NY - 1) + nz + nz - 1 + nz * (NY - 1) + nf - 1) + nf - 1 + 2 * (nf + NY + nz - 3)
+    copies = 2 * (half * (NY - 1) + nz + nz - 1 + nz * (NY - 1) + nf - 1) + nf - 1 + (nf + NY + nz - 3) + (NY * nf + nz - 2)
     vmem = pltpu.VMEM
     scratch = {
         "T": vmem((NY * nz, rows, 256), bf16),
@@ -378,10 +374,11 @@
         scratch["G" + tag] = vmem((NY, nz, 2, 64, 128), bf16)
         scratch["up" + tag] = vmem((nf, 64, 128), bf16)
         scratch["ur" + tag] = vmem((nf, 64, 128), bf16)
-    for tag in ("a", "b"):
-        scratch["sc" + tag] = vmem((4, 8, 128), f32)
-        for stage, n in enumerate((nf, NY, nz)):
-            scratch["sr%d" % stage + tag] = vmem((n, 8, 128), f32)
+    size = {"f": nf, "y": NY, "z": nz, "yf": NY * nf}
+    for tag, stages in STAGES.items():
+        scratch["sc" + tag] = vmem((len(stages) + 1, 8, 128), f32)
+        for stage, group in enumerate(stages):
+            scratch["sr%d" % stage + tag] = vmem((size[group], 8, 128), f32)
     whole = pl.BlockSpec(memory_space=pltpu.VMEM)
     out = pl.pallas_call(
         functools.partial(kernel, nz, nf, float(pairs * nf) ** -0.5),

time: 132 us -> 130 us (0.985)
  Pallas kernels: 128 us -> 126 us
    pallas_call x1, Pallas kernels: 128 us -> 126 us  [per_device(): pl.pallas_call(functools.partial(kernel, nz, nf, float(pairs * nf) ** (-0...]
where the time goes in v3:
time: 130 us; the launch traced here: 129 us
  Pallas kernels  126 us (97%)
  local copies, waits for them, and re-layouts  3.11 us (2%)
    pallas_call x1, Pallas kernels, per_device(): pl.pallas_call(functools.partial(kernel, nz, nf, float(pairs * nf) ** (-0...  126 us
    unnamed x1, local copies, waits for them, and re-layouts  3.11 us

profile of v3, /device:TPU:1, one launch (start us, length us, event | category | flops | bytes accessed | tf_op | source)
XLA Modules:
  0.0 129.5 jit_solution(5462622582252669842)
XLA Ops:
  0.7 125.7 %shard_map.46 = f32[2,64,4096]{2,1,0:T(8,128)} custom-call(s32[1]{0:T(128)S(6)} %copy.6.count_ref, bf16[1024,128]{1,0:T(8,128)(2,1)} %x_ref.1, bf16[128,4096]{1,0:T(8,128)(2,1)} %w_ref.1, bf16[64,1024]{1,0:T(8,128)(2,1)} %bitcast.3), custom_call_target="tpu_custom_call" | custom-call | flops 3221225472 | bytes 4194304 | tf_op jit(solution)/shard_map/pallas_call | solution.py:383
  126.4 3.1 %copy.7 = f32[2,4096,64]{1,2,0:T(8,128)} copy(f32[2,4096,64]{1,2,0:T(8,128)} %bitcast.2) | data formatting | bytes 4194304

commit v4 on v3

--- a/solution.py
+++ b/solution.py
@@ -60,7 +60,6 @@
     to_y = [at_y((y + d) % NY) for d in range(1, NY)]
     to_z = [at_z((z + d) % nz) for d in range(1, nz)]
     to_yf = [(z * NY + (y + j) % NY, (me + d) % nf) for j in range(NY) for d in range(nf) if j + d]
-    far_first = sorted(range(1, nz), key=lambda d: -min(d, nz - d))
 
     barrier = pltpu.get_barrier_semaphore()
     peers = to_yf + to_z
@@ -96,13 +95,22 @@
         out, own, r1, tot, zr = (s[k + tag] for k in ("out", "own", "r1", "tot", "zr"))
         base_y, base_z = take(half * (NY - 1)), take(nz)
 
-        def store(k, j, h, v, more):
+        def store(k, j, h, v, more=True):
             for c in range(2):
-                part = v[:, 128 * c:128 * c + 128]
-                ref = out.at[j, k, h, c] if j < NY - 1 else own.at[k, h, c]
-                if more:
-                    part = part + ref[...].astype(f32)
-                ref[...] = part.astype(ref.dtype)
+                value = v[:, 128 * c:128 * c + 128]
+                if tag == "b":
+                    if more:
+                        value = value + s["part"][h, c]
+                    else:
+                        s["part"][h, c] = value
+                        continue
+                if j == NY - 1:
+                    own[k, h, c] = value
+                    continue
+                high = value.astype(bf16)
+                out[j, k, h, c] = high
+                if tag == "b":
+                    s["lo"][j, k, h, c] = (value - high.astype(f32)).astype(bf16)
 
         def y_copy(k, j):
             return remote(out.at[j, k], r1.at[j, k], to_y[j], base_y + k * (NY - 1) + j)
@@ -118,7 +126,10 @@
 
         def send_z(k, h, d):
             for c, v in enumerate(sum_y(k, h)):
-                tot[d, c] = v.astype(tot.dtype)
+                high = v.astype(bf16)
+                tot[d, c] = high
+                if tag == "b":
+                    s["tl"][d, c] = v - high.astype(f32)
             z_copy(d).start()
 
         def wait_y(k):
@@ -200,7 +211,7 @@
         def batch(k, _):
             for j in range(NY):
                 for h, chunk in enumerate(chunks(k, j)):
-                    store(k, j, h, jnp.dot(rhs[...], T[chunk], preferred_element_type=f32), False)
+                    store(k, j, h, jnp.dot(rhs[...], T[chunk], preferred_element_type=f32))
                 if j < NY - 1:
                     y_copy(k, j).start()
             return 0
@@ -215,33 +226,82 @@
         lax.fori_loop(0, half - 1, sums, 0)
         return last()
 
-    def forward(G, which, first=False):
-        v = None
-        for yd, zd in which:
-            g = jnp.concatenate([G[yd, zd, 0], G[yd, zd, 1]], axis=1)
-            t = nt_dot(T[yd * nz + zd], g)
-            v = t if v is None else v + t
-        v = v.T
-        for h in range(nf):
-            part = v[:, 128 * h:128 * h + 128]
-            acc[h] = part if first else acc[h] + part
+    def send_low():
+        return [push(s["lo"].at[j], s["lr"].at[j], to_y[j]) for j in range(NY - 1)]
+
+    def low_of(k, h, c):
+        return sum(s["lr"][j, k, h, c].astype(f32) for j in range(NY - 1))
+
+    def pass_low(copies):
+        for copy in copies:
+            copy.wait_recv()
+        landing = []
+        for d in range(1, nz):
+            k, h = (d - half, 0) if d >= half else (half - 1 - d, 1)
+            for c in range(2):
+                s["zl"][d, c] = (s["tl"][d, c] + low_of(k, h, c)).astype(bf16)
+            landing.append(push(s["zl"].at[d], s["zlr"].at[d], to_z[d - 1]))
+        return landing
+
+    def end_low(landing):
+        value = [low_of(half - 1, 1, c) for c in range(2)]
+        for d, copy in enumerate(landing):
+            copy.wait_recv()
+            value = [value[c] + s["zlr"][d + 1, c].astype(f32) for c in range(2)]
+        return value
 
     def gather_forward(tag, value):
         G = s["G" + tag]
+        base_z, base_y = take(nz), take(nz * (NY - 1))
         for c in range(2):
             G[y, z, c] = value[c].astype(bf16)
-        landing = [push(G.at[y, z], G.at[y, z], to_z[d - 1]) for d in far_first]
-        across = [[push(G.at[y, z], G.at[y, z], peer) for peer in to_y]]
-        forward(G, [(y, z)], True)
-        for copy, d in zip(landing, far_first):
-            zd = (z - d + nz) % nz
-            copy.wait_recv()
-            across.append([push(G.at[y, zd], G.at[y, zd], peer) for peer in to_y])
-            forward(G, [(y, zd)])
-        for copies, d in zip(across, [0] + far_first):
-            for copy in copies:
-                copy.wait_recv()
-            forward(G, [((y - j + NY) % NY, (z - d + nz) % nz) for j in range(1, NY)])
+
+        def distance(i):
+            return half + (2 * (i % 2) - 1) * (i // 2)
+
+        def z_copy(i):
+            return remote(G.at[y, z], G.at[y, z], at_z((z + distance(i)) % nz), base_z + i)
+
+        def y_copy(i, zd, j):
+            return remote(G.at[y, zd], G.at[y, zd], to_y[j], base_y + i * (NY - 1) + j)
+
+        for i in range(1, nz):
+            z_copy(i).start()
+        for j in range(NY - 1):
+            y_copy(0, z, j).start()
+        acc[...] = jnp.zeros_like(acc)
+
+        def pass_on(i, _):
+            z_copy(i).wait_recv()
+            for j in range(NY - 1):
+                y_copy(i, (z - distance(i) + nz) % nz, j).start()
+            return 0
+
+        lax.fori_loop(1, nz, pass_on, 0)
+
+        def forward(i, _):
+            zd = jnp.where(i == 0, z, (z - distance(i) + nz) % nz)
+            v = None
+            for yd in range(NY):
+                if yd < NY - 1:
+                    y_copy(i, zd, yd).wait_recv()
+            for yd in range(NY):
+                g = jnp.concatenate([G[yd, zd, 0], G[yd, zd, 1]], axis=1)
+                t = nt_dot(T[yd * nz + zd], g)
+                v = t if v is None else v + t
+            v = v.T
+            for h in range(nf):
+                acc[h] = acc[h] + v[:, 128 * h:128 * h + 128]
+            return 0
+
+        lax.fori_loop(0, nz, forward, 0)
+        for i in range(nz):
+            for j in range(NY - 1):
+                pending.append(y_copy(i, z, j))
+            if i:
+                pending.append(z_copy(i))
+        if tag == "b":
+            ends.append(send_low())
         up, ur = s["up" + tag], s["ur" + tag]
         arriving = []
         for d in range(1, nf):
@@ -286,6 +346,7 @@
     s["sca"][0] = jnp.zeros((8, 128), f32)
     s["scb"][0] = jnp.zeros((8, 128), f32)
 
+    ends = []
     b = features_back("b")
     for c in range(2):
         s["bf"][c] = b[c]
@@ -302,21 +363,24 @@
         s["yb"][:, 128 * k:128 * k + 128] = s["ui"][k]
     finish()
     finish = scalar_stage("a", 1, to_y)
-    ends = []
 
     def between():
         finish()
         ends.append(scalar_stage("a", 2, to_z))
+        ends.append(pass_low(ends[0]))
 
     g = only_back("g", s["yb"], between)
-    ends[0]()
+    ends[1]()
+    low = end_low(ends[2])
     rr, uu = unpack("a", 2)
     alpha0 = rr / (uu + RIDGE * rr)
-    b = [s["bf"][c] for c in range(2)]
+    b = [s["bf"][c] + low[c] for c in range(2)]
     r = [(1.0 - RIDGE * alpha0) * b[c] - alpha0 * g[c] for c in range(2)]
     for c in range(2):
+        s["bf"][c] = b[c]
         s["rf"][c] = r[c]
-    v = gather_forward("g", r)
+    part = jnp.minimum(1.0, 2.0 * alpha0)
+    v = gather_forward("g", [r[c] + part * (b[c] - s["Gb"][y, z, c].astype(f32)) for c in range(2)])
     u = s["uf"][...]
     b = [s["bf"][c] for c in range(2)]
     r = [s["rf"][c] for c in range(2)]
@@ -350,7 +414,7 @@
     rows, pairs = inputs.shape[0], freqs.shape[1]
     f32, bf16 = jnp.float32, jnp.bfloat16
     half = nz // 2
-    copies = 2 * (half * (NY - 1) + nz + nz - 1 + nz * (NY - 1) + nf - 1) + nf - 1 + (nf + NY + nz - 3) + (NY * nf + nz - 2)
+    copies = NY + nz + 2 * (half * (NY - 1) + 2 * nz + nz * (NY - 1) + nf - 1) + nf - 1 + (nf + NY + nz - 3) + (NY * nf + nz - 2)
     vmem = pltpu.VMEM
     scratch = {
         "T": vmem((NY * nz, rows, 256), bf16),
@@ -365,12 +429,17 @@
         "send": pltpu.SemaphoreType.DMA((copies,)),
         "recv": pltpu.SemaphoreType.DMA((copies,)),
     }
-    for tag, kind in (("b", f32), ("g", bf16)):
-        scratch["out" + tag] = vmem((NY - 1, half, 2, 2, 64, 128), kind)
+    for name, kind in (("lo", bf16), ("lr", bf16)):
+        scratch[name] = vmem((NY - 1, half, 2, 2, 64, 128), kind)
+    for name, kind in (("tl", f32), ("zl", bf16), ("zlr", bf16)):
+        scratch[name] = vmem((nz, 2, 64, 128), kind)
+    scratch["part"] = vmem((2, 2, 64, 128), f32)
+    for tag in ("b", "g"):
+        scratch["out" + tag] = vmem((NY - 1, half, 2, 2, 64, 128), bf16)
         scratch["own" + tag] = vmem((half, 2, 2, 64, 128), f32)
-        scratch["r1" + tag] = vmem((NY - 1, half, 2, 2, 64, 128), kind)
-        scratch["tot" + tag] = vmem((nz, 2, 64, 128), kind)
-        scratch["zr" + tag] = vmem((nz, 2, 64, 128), kind)
+        scratch["r1" + tag] = vmem((NY - 1, half, 2, 2, 64, 128), bf16)
+        scratch["tot" + tag] = vmem((nz, 2, 64, 128), bf16)
+        scratch["zr" + tag] = vmem((nz, 2, 64, 128), bf16)
         scratch["G" + tag] = vmem((NY, nz, 2, 64, 128), bf16)
         scratch["up" + tag] = vmem((nf, 64, 128), bf16)
         scratch["ur" + tag] = vmem((nf, 64, 128), bf16)

time: 130 us -> 123 us (0.946)
  Pallas kernels: 126 us -> 119 us
    pallas_call x1, Pallas kernels: 126 us -> 119 us  [per_device(): pl.pallas_call(functools.partial(kernel, nz, nf, float(pairs * nf) ** (-0...]
where the time goes in v4:
time: 123 us
  Pallas kernels  119 us (97%)
  local copies, waits for them, and re-layouts  3.11 us (3%)
    pallas_call x1, Pallas kernels, per_device(): pl.pallas_call(functools.partial(kernel, nz, nf, float(pairs * nf) ** (-0...  119 us
    unnamed x1, local copies, waits for them, and re-layouts  3.11 us

profile of v4, /device:TPU:1, one launch (start us, length us, event | category | flops | bytes accessed | tf_op | source)
XLA Modules:
  0.0 122.8 jit_solution(3201835907127120257)
XLA Ops:
  0.7 119.0 %shard_map.46 = f32[2,64,4096]{2,1,0:T(8,128)} custom-call(s32[1]{0:T(128)S(6)} %copy.6.count_ref, bf16[1024,128]{1,0:T(8,128)(2,1)} %x_ref.1, bf16[128,4096]{1,0:T(8,128)(2,1)} %w_ref.1, bf16[64,1024]{1,0:T(8,128)(2,1)} %bitcast.3), custom_call_target="tpu_custom_call" | custom-call | flops 3221225472 | bytes 4194304 | tf_op jit(solution)/shard_map/pallas_call | solution.py:452
  119.7 3.1 %copy.7 = f32[2,4096,64]{1,2,0:T(8,128)} copy(f32[2,4096,64]{1,2,0:T(8,128)} %bitcast.2) | data formatting | bytes 4194304

commit v5 on v4

--- a/solution.py
+++ b/solution.py
@@ -203,6 +203,7 @@
         lax.fori_loop(0, half, batch, 0)
         for i in range(2):
             back(half - 1, NY - 1, i)
+        ends.append(send_low())
         return last()
 
     def only_back(tag, rhs, between):
@@ -300,14 +301,14 @@
                 pending.append(y_copy(i, z, j))
             if i:
                 pending.append(z_copy(i))
-        if tag == "b":
-            ends.append(send_low())
         up, ur = s["up" + tag], s["ur" + tag]
         arriving = []
         for d in range(1, nf):
             to = (me + d) % nf
             up[d] = acc[to].astype(up.dtype)
             arriving.append(push(up.at[d], ur.at[d], at_f(to)))
+        if tag == "b":
+            ends.append(pass_low(ends[0]))
         total = acc[me]
         for d, copy in enumerate(arriving):
             copy.wait_recv()
@@ -367,11 +368,10 @@
     def between():
         finish()
         ends.append(scalar_stage("a", 2, to_z))
-        ends.append(pass_low(ends[0]))
 
     g = only_back("g", s["yb"], between)
-    ends[1]()
-    low = end_low(ends[2])
+    ends[2]()
+    low = end_low(ends[1])
     rr, uu = unpack("a", 2)
     alpha0 = rr / (uu + RIDGE * rr)
     b = [s["bf"][c] + low[c] for c in range(2)]

time: 123 us -> 121 us (0.984)
  Pallas kernels: 119 us -> 117 us
    pallas_call x1, Pallas kernels: 119 us -> 117 us  [per_device(): pl.pallas_call(functools.partial(kernel, nz, nf, float(pairs * nf) ** (-0...]
where the time goes in v5:
time: 121 us
  Pallas kernels  117 us (97%)
  local copies, waits for them, and re-layouts  3.11 us (3%)
    pallas_call x1, Pallas kernels, per_device(): pl.pallas_call(functools.partial(kernel, nz, nf, float(pairs * nf) ** (-0...  117 us
    unnamed x1, local copies, waits for them, and re-layouts  3.11 us

profile of v5, /device:TPU:1, one launch (start us, length us, event | category | flops | bytes accessed | tf_op | source)
XLA Modules:
  0.0 121.0 jit_solution(5545628935895470838)
XLA Ops:
  0.7 117.2 %shard_map.46 = f32[2,64,4096]{2,1,0:T(8,128)} custom-call(s32[1]{0:T(128)S(6)} %copy.6.count_ref, bf16[1024,128]{1,0:T(8,128)(2,1)} %x_ref.1, bf16[128,4096]{1,0:T(8,128)(2,1)} %w_ref.1, bf16[64,1024]{1,0:T(8,128)(2,1)} %bitcast.3), custom_call_target="tpu_custom_call" | custom-call | flops 3221225472 | bytes 4194304 | tf_op jit(solution)/shard_map/pallas_call | solution.py:452
  117.9 3.1 %copy.7 = f32[2,4096,64]{1,2,0:T(8,128)} copy(f32[2,4096,64]{1,2,0:T(8,128)} %bitcast.2) | data formatting | bytes 4194304

commit v6 on v5

--- a/solution.py
+++ b/solution.py
@@ -258,7 +258,7 @@
             G[y, z, c] = value[c].astype(bf16)
 
         def distance(i):
-            return half + (2 * (i % 2) - 1) * (i // 2)
+            return (i % 2) * ((i + 1) // 2) + (1 - i % 2) * (nz - i // 2)
 
         def z_copy(i):
             return remote(G.at[y, z], G.at[y, z], at_z((z + distance(i)) % nz), base_z + i)
@@ -266,7 +266,7 @@
         def y_copy(i, zd, j):
             return remote(G.at[y, zd], G.at[y, zd], to_y[j], base_y + i * (NY - 1) + j)
 
-        for i in range(1, nz):
+        for i in (nz - 1, *range(1, nz - 1)):
             z_copy(i).start()
         for j in range(NY - 1):
             y_copy(0, z, j).start()

time: 121 us -> 121 us (level)
  no operation moved by 1% of the time
where the time goes in v6:
time: 121 us
  Pallas kernels  117 us (97%)
  local copies, waits for them, and re-layouts  3.11 us (3%)
    pallas_call x1, Pallas kernels, per_device(): pl.pallas_call(functools.partial(kernel, nz, nf, float(pairs * nf) ** (-0...  117 us
    unnamed x1, local copies, waits for them, and re-layouts  3.11 us

profile of v6, /device:TPU:1, one launch (start us, length us, event | category | flops | bytes accessed | tf_op | source)
XLA Modules:
  0.0 120.7 jit_solution(8356651210200272251)
XLA Ops:
  0.7 116.9 %shard_map.46 = f32[2,64,4096]{2,1,0:T(8,128)} custom-call(s32[1]{0:T(128)S(6)} %copy.6.count_ref, bf16[1024,128]{1,0:T(8,128)(2,1)} %x_ref.1, bf16[128,4096]{1,0:T(8,128)(2,1)} %w_ref.1, bf16[64,1024]{1,0:T(8,128)(2,1)} %bitcast.3), custom_call_target="tpu_custom_call" | custom-call | flops 3221225472 | bytes 4194304 | tf_op jit(solution)/shard_map/pallas_call | solution.py:452
  117.6 3.1 %copy.7 = f32[2,4096,64]{1,2,0:T(8,128)} copy(f32[2,4096,64]{1,2,0:T(8,128)} %bitcast.2) | data formatting | bytes 4194304
